TPU v7x, 512 devices: a whole 4x4x16 slice. The times are simulated.
512 devices in a mesh: expert: 32 (over z, core), fsdp: 16 (over y, x).
Axes of the slice: x: 4, y: 4, z: 16, core: 2. Of those that a mesh axis runs over, the one named last changes fastest.
Arguments:
- tokens: bfloat16 [1024, 4096], P('expert', 'fsdp'), may hold values from -6 to 6
- cotangent: bfloat16 [1024, 4096], P('expert', 'fsdp'), may hold values from -6 to 6
- expert_ids: int32 [1024, 8], P('expert'), may hold values from 0 to 31, as said below
- gate_logits: float32 [1024, 8], P('expert'), may hold values from -6 to 6
- shadow_plan: int32 [32], replicated, may hold values from 0 to 1, as said below
- w_in: bfloat16 [32, 4096, 2, 768], P('expert', 'fsdp'), may hold values from -0.09375 to 0.09375
- w_out: bfloat16 [32, 768, 4096], P('expert', None, 'fsdp'), may hold values from -0.21875 to 0.21875
- mom_in: bfloat16 [32, 4096, 2, 768], P('expert', 'fsdp'), may hold values from -3 to 3
- mom_out: bfloat16 [32, 768, 4096], P('expert', None, 'fsdp'), may hold values from -3 to 3
- in_rows: float32 [32, 2, 4096], P('expert', None, 'fsdp'), may hold values from 1e-05 to 0.01
- in_cols: float32 [32, 2, 2, 768], P('expert'), may hold values from 1e-05 to 0.01
- out_rows: float32 [32, 2, 768], P('expert'), may hold values from 1e-05 to 0.01
- out_cols: float32 [32, 2, 4096], P('expert', None, 'fsdp'), may hold values from 1e-05 to 0.01
Outputs:
- output: bfloat16 [1024, 4096], P('expert', 'fsdp')
- grad_tokens: bfloat16 [1024, 4096], P('expert', 'fsdp')
- new_w_in: bfloat16 [32, 4096, 2, 768], P('expert', 'fsdp')
- new_w_out: bfloat16 [32, 768, 4096], P('expert', None, 'fsdp')
- new_mom_in: bfloat16 [32, 4096, 2, 768], P('expert', 'fsdp')
- new_mom_out: bfloat16 [32, 768, 4096], P('expert', None, 'fsdp')
- new_in_rows: float32 [32, 2, 4096], P('expert', None, 'fsdp')
- new_in_cols: float32 [32, 2, 2, 768], P('expert')
- new_out_rows: float32 [32, 2, 768], P('expert')
- new_out_cols: float32 [32, 2, 4096], P('expert', None, 'fsdp')
Inputs may be any that keep to these rules, and one draw needn't show every extreme that they name: `expert_ids`: each row names 8 different experts. `shadow_plan`: exactly 4 entries are 1, one in every run of 8 consecutive experts starting at expert 0, all at the same position within their run; the others 0.
All inputs are finite; a program needn't handle non-finite values.
Results may differ from a plain program's by a relative error of at most 0.0064.
Values may be sent and summed in bfloat16 or wider, within the bound.
A program may use at most 128 MiB of HBM per device.

v0:
```python
import jax
import jax.numpy as jnp
from jax import lax
from jax.sharding import PartitionSpec as P

BETA_ONE = 0.9
BETA_TWO = 0.999
BETA_THREE = 0.9999
EPS_ONE = 1e-30
EPS_TWO = 1e-16
CLIP_LIMIT = 1.0
LEARN_RATE = 0.01


def slot_plan(expert_ids, shadow_plan, capacity):
    flat_ids = expert_ids.reshape(-1)
    expert_count = shadow_plan.shape[0]
    one_hot = (flat_ids[:, None] == jnp.arange(expert_count, dtype=jnp.int32)[None, :]).astype(
        jnp.int32
    )
    earlier = jnp.cumsum(one_hot, axis=0) - one_hot
    slot_rank = jnp.sum(earlier * one_hot, axis=1)
    is_hot = jnp.sum(one_hot * shadow_plan[None, :], axis=1)
    kept_mask = (slot_rank < capacity) | (is_hot > 0) & (slot_rank < 2 * capacity)
    return (flat_ids, slot_rank, kept_mask)


def spread_rows(pair_rows, slot_index, total_slots):
    buffer = jnp.zeros((total_slots, pair_rows.shape[1]), pair_rows.dtype)
    return buffer.at[slot_index].set(pair_rows, mode="drop")


def per_block(source, weight_sets, product):
    pieces = []
    for row_lower, row_upper, weight_in, weight_out in weight_sets:
        pieces.append(product(source, weight_in, weight_out))
    return pieces[0]


def per_device(
    tokens,
    cotangent,
    expert_ids,
    gate_logits,
    shadow_plan,
    w_in,
    w_out,
    mom_in,
    mom_out,
    in_rows,
    in_cols,
    out_rows,
    out_cols,
):
    groups = lax.axis_size("expert")
    fsdp_count = lax.axis_size("fsdp")
    tok_rows, topk_width = expert_ids.shape
    feat_local = tokens.shape[1]
    ff_width = w_in.shape[3]
    full_rows = feat_local * fsdp_count
    capacity = tok_rows * topk_width // groups
    flat_ids, slot_rank, kept_mask = slot_plan(expert_ids, shadow_plan, capacity)
    home_in = w_in[0].reshape(feat_local, 2 * ff_width)
    home_out = w_out[0]
    slots = 2 * capacity
    weight_sets = [(0, slots, home_in, home_out)]
    total_slots = groups * slots
    slot_index = jnp.where(kept_mask, flat_ids * slots + slot_rank, total_slots)
    read_index = jnp.minimum(slot_index, total_slots - 1)
    sig_logits = jax.nn.sigmoid(gate_logits)
    gates = sig_logits / jnp.sum(sig_logits, axis=1, keepdims=True)
    pair_gate = jnp.where(kept_mask, gates.reshape(-1), 0.0)
    sent_rows = spread_rows(jnp.repeat(tokens, topk_width, axis=0), slot_index, total_slots)
    received = lax.all_to_all(
        sent_rows.reshape(groups, slots, feat_local),
        "expert",
        split_axis=0,
        concat_axis=0,
        tiled=True,
    )

    def gate_up_part(block, weight_in, weight_out):
        return jnp.dot(
            block.reshape(-1, feat_local), weight_in, preferred_element_type=jnp.float32
        ).reshape(groups, block.shape[1], 2, ff_width)

    partial_sums = per_block(received, weight_sets, gate_up_part)
    gate_up = lax.psum_scatter(partial_sums, "fsdp", scatter_dimension=3, tiled=True)
    gate_pre = gate_up[:, :, 0]
    up_pre = gate_up[:, :, 1]
    hidden_local = (gate_pre * jax.nn.sigmoid(gate_pre) * up_pre).astype(jnp.bfloat16)
    hidden_full = lax.all_gather(hidden_local, "fsdp", axis=2, tiled=True)

    def down_part(block, weight_in, weight_out):
        return jnp.dot(
            block.reshape(-1, ff_width), weight_out, preferred_element_type=jnp.float32
        ).reshape(groups, block.shape[1], feat_local)

    expert_out = per_block(hidden_full, weight_sets, down_part).astype(jnp.bfloat16)
    returned = lax.all_to_all(
        expert_out, "expert", split_axis=0, concat_axis=0, tiled=True
    ).reshape(total_slots, feat_local)
    pair_out = returned[read_index].astype(jnp.float32) * pair_gate[:, None]
    output = jnp.sum(pair_out.reshape(tok_rows, topk_width, feat_local), axis=1).astype(
        jnp.bfloat16
    )
    pair_cot = (
        jnp.repeat(cotangent, topk_width, axis=0).astype(jnp.float32) * pair_gate[:, None]
    ).astype(jnp.bfloat16)
    sent_cot = spread_rows(pair_cot, slot_index, total_slots)
    out_grad = lax.all_to_all(
        sent_cot.reshape(groups, slots, feat_local),
        "expert",
        split_axis=0,
        concat_axis=0,
        tiled=True,
    )

    def hidden_grad_part(block, weight_in, weight_out):
        return jnp.dot(
            block.reshape(-1, feat_local), weight_out.T, preferred_element_type=jnp.float32
        ).reshape(groups, block.shape[1], ff_width)

    hidden_grad = lax.psum_scatter(
        per_block(out_grad, weight_sets, hidden_grad_part), "fsdp", scatter_dimension=2, tiled=True
    )
    gate_sig = jax.nn.sigmoid(gate_pre)
    gate_grad = hidden_grad * up_pre * gate_sig * (1.0 + gate_pre * (1.0 - gate_sig))
    up_grad = hidden_grad * gate_pre * gate_sig
    pre_grad = jnp.stack([gate_grad, up_grad], axis=2).astype(jnp.bfloat16)
    pre_grad_full = lax.all_gather(pre_grad, "fsdp", axis=3, tiled=True)

    def input_grad_part(block, weight_in, weight_out):
        return jnp.dot(
            block.reshape(-1, 2 * ff_width), weight_in.T, preferred_element_type=jnp.float32
        ).reshape(groups, block.shape[1], feat_local)

    in_grad = per_block(pre_grad_full, weight_sets, input_grad_part).astype(jnp.bfloat16)
    returned_grad = lax.all_to_all(
        in_grad, "expert", split_axis=0, concat_axis=0, tiled=True
    ).reshape(total_slots, feat_local)
    kept_float = kept_mask.astype(jnp.float32)
    pair_grad = returned_grad[read_index].astype(jnp.float32) * kept_float[:, None]
    grad_tokens = jnp.sum(pair_grad.reshape(tok_rows, topk_width, feat_local), axis=1).astype(
        jnp.bfloat16
    )
    block_in = received.reshape(-1, feat_local)
    block_pre = pre_grad_full.reshape(-1, 2 * ff_width)
    block_hidden = hidden_full.reshape(-1, ff_width)
    block_out = out_grad.reshape(-1, feat_local)
    grad_in = jnp.dot(block_in.T, block_pre, preferred_element_type=jnp.float32)
    grad_out = jnp.dot(block_hidden.T, block_out, preferred_element_type=jnp.float32)
    sq_in = grad_in * grad_in + EPS_ONE
    sq_out = grad_out * grad_out + EPS_ONE
    row_v_in = BETA_TWO * in_rows[0, 0] + (1.0 - BETA_TWO) * jnp.mean(sq_in, axis=1)
    col_v_out = BETA_TWO * out_cols[0, 0] + (1.0 - BETA_TWO) * jnp.mean(sq_out, axis=0)
    col_sq_in, row_sq_out, row_v_in_sum = lax.psum(
        (jnp.sum(sq_in, axis=0), jnp.sum(sq_out, axis=1), jnp.sum(row_v_in)), "fsdp"
    )
    col_v_in = BETA_TWO * in_cols[0, 0].reshape(-1) + (1.0 - BETA_TWO) * col_sq_in / full_rows
    row_v_out = BETA_TWO * out_rows[0, 0] + (1.0 - BETA_TWO) * row_sq_out / full_rows
    scaled_in = grad_in / jnp.sqrt(
        row_v_in[:, None] * col_v_in[None, :] / (row_v_in_sum / full_rows)
    )
    scaled_out = grad_out / jnp.sqrt(row_v_out[:, None] * col_v_out[None, :] / jnp.mean(row_v_out))
    norm_in, norm_out = lax.psum(
        (jnp.sum(scaled_in * scaled_in), jnp.sum(scaled_out * scaled_out)), "fsdp"
    )
    scaled_in = scaled_in / jnp.maximum(
        1.0, jnp.sqrt(norm_in / (full_rows * 2 * ff_width)) / CLIP_LIMIT
    )
    scaled_out = scaled_out / jnp.maximum(
        1.0, jnp.sqrt(norm_out / (ff_width * full_rows)) / CLIP_LIMIT
    )
    moment_in = (
        BETA_ONE * mom_in[0].reshape(feat_local, 2 * ff_width).astype(jnp.float32)
        + (1.0 - BETA_ONE) * scaled_in
    )
    moment_out = BETA_ONE * mom_out[0].astype(jnp.float32) + (1.0 - BETA_ONE) * scaled_out
    residue_in = (scaled_in - moment_in) * (scaled_in - moment_in) + EPS_TWO
    residue_out = (scaled_out - moment_out) * (scaled_out - moment_out) + EPS_TWO
    row_r_in = BETA_THREE * in_rows[0, 1] + (1.0 - BETA_THREE) * jnp.mean(residue_in, axis=1)
    col_r_out = BETA_THREE * out_cols[0, 1] + (1.0 - BETA_THREE) * jnp.mean(residue_out, axis=0)
    col_res_in, row_res_out, row_r_in_sum = lax.psum(
        (jnp.sum(residue_in, axis=0), jnp.sum(residue_out, axis=1), jnp.sum(row_r_in)), "fsdp"
    )
    col_r_in = BETA_THREE * in_cols[0, 1].reshape(-1) + (1.0 - BETA_THREE) * col_res_in / full_rows
    row_r_out = BETA_THREE * out_rows[0, 1] + (1.0 - BETA_THREE) * row_res_out / full_rows
    step_in = moment_in / jnp.sqrt(
        row_r_in[:, None] * col_r_in[None, :] / (row_r_in_sum / full_rows)
    )
    step_out = moment_out / jnp.sqrt(row_r_out[:, None] * col_r_out[None, :] / jnp.mean(row_r_out))
    new_w_in = (
        (home_in.astype(jnp.float32) - LEARN_RATE * step_in)
        .astype(jnp.bfloat16)
        .reshape(1, feat_local, 2, ff_width)
    )
    new_w_out = (home_out.astype(jnp.float32) - LEARN_RATE * step_out).astype(jnp.bfloat16)[None]
    new_mom_in = moment_in.astype(jnp.bfloat16).reshape(1, feat_local, 2, ff_width)
    new_mom_out = moment_out.astype(jnp.bfloat16)[None]
    new_in_rows = jnp.stack([row_v_in, row_r_in])[None]
    new_in_cols = jnp.stack([col_v_in, col_r_in]).reshape(1, 2, 2, ff_width)
    new_out_rows = jnp.stack([row_v_out, row_r_out])[None]
    new_out_cols = jnp.stack([col_v_out, col_r_out])[None]
    return (
        output,
        grad_tokens,
        new_w_in,
        new_w_out,
        new_mom_in,
        new_mom_out,
        new_in_rows,
        new_in_cols,
        new_out_rows,
        new_out_cols,
    )


def solution(mesh):
    return jax.shard_map(
        per_device,
        mesh=mesh,
        in_specs=(
            P("expert", "fsdp"),
            P("expert", "fsdp"),
            P("expert", None),
            P("expert", None),
            P(),
            P("expert", "fsdp", None, None),
            P("expert", None, "fsdp"),
            P("expert", "fsdp", None, None),
            P("expert", None, "fsdp"),
            P("expert", None, "fsdp"),
            P("expert", None, None, None),
            P("expert", None, None),
            P("expert", None, "fsdp"),
        ),
        out_specs=(
            P("expert", "fsdp"),
            P("expert", "fsdp"),
            P("expert", "fsdp", None, None),
            P("expert", None, "fsdp"),
            P("expert", "fsdp", None, None),
            P("expert", None, "fsdp"),
            P("expert", None, "fsdp"),
            P("expert", None, None, None),
            P("expert", None, None),
            P("expert", None, "fsdp"),
        ),
        check_vma=False,
    )
```

profile of v0, /device:TPU:32, one launch (start us, length us, event | category | flops | bytes accessed | tf_op | source)
XLA Modules:
  0.0 580.8 jit_solution(13759671450555457203)
XLA Ops:
  9.9 0.8 copy.48
  12.5 1.6 scatter_custom_fusion.1
  14.1 36.1 %all_to_all.20 = bf16[32,16,256]{2,1,0:T(8,128)(2,1)S(1)} all-to-all(bf16[32,16,256]{2,1,0:T(8,128)(2,1)S(1)} %bitcast.191), channel_id=1, replica_groups=mesh['expert'=32,'fsdp'=16] {'expert'}, dimensions={0} | all-to-all | bytes 524288 | tf_op jit(solution)/shard_map/all_to_all | solution.py:111
  50.9 1.4 fusion.6
  52.3 10.4 %copy.57 = f32[32,16,768]{1,0,2:T(8,128)} copy(f32[32,16,768]{2,1,0:T(8,128)S(1)} %fusion.6) | data formatting | bytes 3145728
  62.7 11.6 %reshape.411 = f32[768,512]{1,0:T(8,128)} reshape(f32[768,32,16]{2,1,0:T(8,128)} %bitcast.176) | data formatting | bytes 3145728
  74.3 2.1 scatter_custom_fusion
  76.5 5.5 all-to-all-start
  82.2 1.2 copy.54
  83.4 19.8 %all-to-all-done = bf16[32,16,256]{2,1,0:T(8,128)(2,1)S(1)} async-done(((bf16[32,16,256]{2,1,0:T(8,128)(2,1)}), bf16[32,16,256]{2,1,0:T(8,128)(2,1)S(1)}, u32[]{:S(2)}, u32[]{:S(2)}) %all-to-all-start) | async-done | bytes 262176 | tf_op jit(solution)/shard_map/all_to_all | solution.py:74
  103.1 1.8 fusion.14
  105.0 23.9 %copy.55 = f32[32,16,2,768]{1,2,0,3:T(2,128)} copy(f32[32,16,2,768]{3,1,2,0:T(8,128)S(1)} %fusion.14) | data formatting | bytes 6291456
  128.9 40.3 %reshape.409 = f32[768,1024]{1,0:T(8,128)} reshape(f32[768,32,2,16]{3,2,1,0:T(2,128)} %bitcast.175) | data formatting | bytes 6291456
  169.5 1.2 reshape.412
  171.1 82.1 %reduce-scatter.7.cloned.1.call-done = f32[48,1024]{1,0:T(8,128)} async-done(((f32[768,1024]{1,0:T(8,128)}), f32[48,1024]{1,0:T(8,128)}) %reduce-scatter.7.cloned.1.call-update) | async-done | bytes 196624
  253.1 3.0 reshape.410
  256.2 1.8 fusion.54
  257.9 0.8 copy.60
  258.8 0.8 copy.61
  259.9 1.4 copy.49
  261.3 2.0 convert_multiply_fusion
  263.5 32.0 %all_gather.6 = bf16[32,16,768]{0,1,2:T(8,128)(2,1)S(1)} all-gather(bf16[32,16,48]{0,1,2:T(8,128)(2,1)S(1)} %copy.46), channel_id=1, replica_groups=mesh['expert'=32,'fsdp'=16] {'fsdp'}, dimensions={2}, use_global_device_ids=true | all-gather | bytes 835584 | tf_op jit(solution)/shard_map/all_gather | solution.py:92
  295.6 3.9 copy.47
  299.5 2.4 convolution_convert_fusion.1
  301.9 12.8 %all-to-all-start.1 = ((bf16[32,16,256]{2,1,0:T(8,128)(2,1)}), bf16[32,16,256]{2,1,0:T(8,128)(2,1)S(1)}, u32[]{:S(2)}, u32[]{:S(2)}) async-start(bf16[32,16,256]{2,1,0:T(8,128)(2,1)} %convolution_convert_fusion.1), calls=%async_computation.1 | async-start | bytes 524288 | tf_op jit(solution)/shard_map/all_to_all | solution.py:100
  314.7 3.1 reshape.406
  318.8 2.5 fusion.2
  321.3 14.4 %all-to-all-done.1 = bf16[32,16,256]{2,1,0:T(8,128)(2,1)S(1)} async-done(((bf16[32,16,256]{2,1,0:T(8,128)(2,1)}), bf16[32,16,256]{2,1,0:T(8,128)(2,1)S(1)}, u32[]{:S(2)}, u32[]{:S(2)}) %all-to-all-start.1) | async-done | bytes 262176 | tf_op jit(solution)/shard_map/all_to_all | solution.py:100
  335.7 1.2 gather_fusion
  336.8 0.8 fusion.13
  337.6 1.7 all-gather.2.cloned.1.call-done
  339.2 10.6 %copy.50 = bf16[32,16,2,768]{3,2,1,0:T(2,128)(2,1)S(1)} copy(bf16[32,16,2,768]{0,1,2,3:T(8,128)(2,1)} %all-gather.2.cloned.1.call-done) | data formatting | bytes 3145728 | tf_op jit(solution)/shard_map/all_gather | solution.py:131
  349.9 1.9 dot_general.29
  354.1 72.4 %all-reduce.2 = (f32[]{:T(128)}, f32[1536]{0:T(1024)S(1)}, f32[768]{0:T(1024)S(1)}) all-reduce(f32[]{:T(128)} %get-tuple-element.38, f32[1536]{0:T(1024)S(1)} %get-tuple-element.12, f32[768]{0:T(1024)S(1)} %get-tuple-element.17), channel_id=1, replica_groups=mesh['expert'=32,'fsdp'=16] {'fsdp'}, use_global_device_ids=true, to_apply=%region_15.16 | all-reduce | flops 2305 | bytes 18440 | tf_op jit(solution)/shard_map/psum | solution.py:157
  427.0 2.9 convolution_convert_fusion
  431.3 1.3 multiply_reduce_fusion
  432.6 0.9 multiply_reduce_fusion.1
  433.5 12.8 %all-to-all-start.3 = ((bf16[32,16,256]{2,1,0:T(8,128)(2,1)}), bf16[32,16,256]{2,1,0:T(8,128)(2,1)S(1)}, u32[]{:S(2)}, u32[]{:S(2)}) async-start(bf16[32,16,256]{2,1,0:T(8,128)(2,1)} %convolution_convert_fusion), calls=%async_computation.3 | async-start | bytes 524288 | tf_op jit(solution)/shard_map/all_to_all | solution.py:139
  446.3 36.1 %all-reduce.1 = (f32[]{:T(128)}, f32[]{:T(128)}) all-reduce(f32[]{:T(128)} %multiply_reduce_fusion, f32[]{:T(128)} %multiply_reduce_fusion.1), channel_id=1, replica_groups=mesh['expert'=32,'fsdp'=16] {'fsdp'}, use_global_device_ids=true, to_apply=%region_17.18 | all-reduce | flops 2 | bytes 16 | tf_op jit(solution)/shard_map/psum | solution.py:166
  483.8 2.4 fusion.5
  486.1 0.9 copy-done.3
  487.3 0.8 fusion.47
  488.8 71.4 %all-reduce = (f32[]{:T(128)}, f32[1536]{0:T(1024)S(1)}, f32[768]{0:T(1024)S(1)}) all-reduce(f32[]{:T(128)} %get-tuple-element.34, f32[1536]{0:T(1024)S(1)} %get-tuple-element.10, f32[768]{0:T(1024)S(1)} %get-tuple-element.15), channel_id=1, replica_groups=mesh['expert'=32,'fsdp'=16] {'fsdp'}, use_global_device_ids=true, to_apply=%region_22.23 | all-reduce | flops 2305 | bytes 18440 | tf_op jit(solution)/shard_map/psum | solution.py:184
  560.8 3.2 fusion.46
  564.0 3.1 reshape.367
  568.4 1.1 reshape.368
  571.3 1.1 fusion.9
  572.4 1.2 gather_fusion.1
  (103 shorter events, 14.4 us)
Async XLA Ops:
  7.2 67.2 %copy-start = (bf16[32,256]{1,0:T(8,128)(2,1)S(1)}, bf16[32,256]{1,0:T(8,128)(2,1)}, u32[]{:S(2)}) copy-start(bf16[32,256]{1,0:T(8,128)(2,1)} %param.13) | copy-start | bytes 49156
  7.2 162.2 %reduce-scatter.9.cloned.1.call-start = ((), (), s32[]{:S(2)}) async-start(), calls=%async_computation.8 | async-start | bytes 1671168
  50.2 0.7 copy-start.14
  74.3 7.8 %copy-start.9 = (bf16[1,256,2,768]{3,2,1,0:T(2,128)(2,1)S(1)}, bf16[1,256,2,768]{3,2,1,0:T(2,128)(2,1)}, u32[]{:S(2)}) copy-start(bf16[1,256,2,768]{3,2,1,0:T(2,128)(2,1)} %param.18) | copy-start | bytes 2359300
  76.5 26.7 %all-to-all-start = ((bf16[32,16,256]{2,1,0:T(8,128)(2,1)}), bf16[32,16,256]{2,1,0:T(8,128)(2,1)S(1)}, u32[]{:S(2)}, u32[]{:S(2)}) async-start(bf16[32,16,256]{2,1,0:T(8,128)(2,1)} %bitcast.4), calls=%async_computation | async-start | bytes 524288 | tf_op jit(solution)/shard_map/all_to_all | solution.py:74
  82.0 171.1 %reduce-scatter.7.cloned.1.call-start = ((), (), s32[]{:S(2)}) async-start(), calls=%async_computation.7 | async-start | bytes 3342336
  82.2 21.0 %copy-start.2 = (bf16[32,8,2,768]{3,1,2,0:T(8,128)(2,1)}, bf16[32,8,2,768]{3,1,2,0:T(8,128)(2,1)S(1)}, u32[]{:S(2)}) copy-start(bf16[32,8,2,768]{3,1,2,0:T(8,128)(2,1)S(1)} %copy.63) | copy-start | bytes 2359300
  103.1 1.8 copy-start.12
  169.2 170.0 %all-gather.2.cloned.1.call-start = ((), (), s32[]{:S(2)}) async-start(), calls=%async_computation.6 | async-start | bytes 6684672 | tf_op jit(solution)/shard_map/all_gather | solution.py:131
  259.6 1.7 copy-start.17
  259.6 1.7 copy-start.18
  259.6 1.7 copy-start.16
  259.6 1.7 copy-start.15
  299.5 18.5 %copy-start.5 = (f32[1,256,2,768]{3,2,1,0:T(2,128)S(1)}, f32[1,256,2,768]{3,2,1,0:T(2,128)}, u32[]{:S(2)}) copy-start(f32[1,256,2,768]{3,2,1,0:T(2,128)} %convert_multiply_fusion) | copy-start | bytes 4718596
  301.9 33.8 %all-to-all-start.1 = ((bf16[32,16,256]{2,1,0:T(8,128)(2,1)}), bf16[32,16,256]{2,1,0:T(8,128)(2,1)S(1)}, u32[]{:S(2)}, u32[]{:S(2)}) async-start(bf16[32,16,256]{2,1,0:T(8,128)(2,1)} %convolution_convert_fusion.1), calls=%async_computation.1 | async-start | bytes 524288 | tf_op jit(solution)/shard_map/all_to_all | solution.py:100
  318.0 0.7 copy-start.19
  351.8 0.9 copy-start.13
  431.3 1.3 copy-start.10
  433.5 138.9 %all-to-all-start.3 = ((bf16[32,16,256]{2,1,0:T(8,128)(2,1)}), bf16[32,16,256]{2,1,0:T(8,128)(2,1)S(1)}, u32[]{:S(2)}, u32[]{:S(2)}) async-start(bf16[32,16,256]{2,1,0:T(8,128)(2,1)} %convolution_convert_fusion), calls=%async_computation.3 | async-start | bytes 524288 | tf_op jit(solution)/shard_map/all_to_all | solution.py:139
  483.8 3.2 copy-start.7
  486.1 0.9 copy-start.3
  564.0 4.4 copy-start.11
  564.0 7.3 %copy-start.4 = (f32[768,256]{1,0:T(8,128)S(1)}, f32[768,256]{1,0:T(8,128)}, u32[]{:S(2)}) copy-start(f32[768,256]{1,0:T(8,128)} %copy-done.3) | copy-start | bytes 2359300
  564.0 7.3 %copy-start.6 = (bf16[1,768,256]{2,1,0:T(8,128)(2,1)S(1)}, bf16[1,768,256]{2,1,0:T(8,128)(2,1)}, u32[]{:S(2)}) copy-start(bf16[1,768,256]{2,1,0:T(8,128)(2,1)} %param.19) | copy-start | bytes 1179652
  564.0 7.3 %copy-start.8 = (bf16[1,768,256]{2,1,0:T(8,128)(2,1)S(1)}, bf16[1,768,256]{2,1,0:T(8,128)(2,1)}, u32[]{:S(2)}) copy-start(bf16[1,768,256]{2,1,0:T(8,128)(2,1)} %param.21) | copy-start | bytes 1179652
  571.3 3.0 copy-start.1
Sparse Core Ops, SparseCore 0:
  74.5 81.8 reduce-scatter.8
  169.3 83.7 reduce-scatter.6
  261.4 77.8 all-gather.1
where the time goes:
time: 582 us; the launch traced here: 581 us
  blocking collectives  248 us (43%)
  local copies, waits for them, and re-layouts  131 us (23%)
  waiting for transfers between devices  118 us (20%)
  starting transfers between devices  31.4 us (5%)
  other arithmetic  22.7 us (4%)
  between operations  18.2 us (3%)
  matrix products  11.8 us (2%)
    unnamed x54, local copies, waits for them, and re-layouts  97.2 us
    unnamed x5, waiting for transfers between devices  82.1 us
    psum x1, blocking collectives, per_device(): lax.psum((jnp.sum(sq_in, axis=0), jnp.sum(sq_out, axis=1), jnp.sum(row_v_...  72.4 us
    psum x1, blocking collectives, per_device(): lax.psum((jnp.sum(residue_in, axis=0), jnp.sum(residue_out, axis=1), jnp....  71.4 us
    all_to_all x1, blocking collectives, per_device(): lax.all_to_all(sent_cot.reshape(groups, slots, feat_local), 'expert', spl...  36.1 us
    psum x1, blocking collectives, per_device(): lax.psum((jnp.sum(scaled_in * scaled_in), jnp.sum(scaled_out * scaled_out...  36.1 us
    all_gather x1, blocking collectives, per_device(): hidden_full = lax.all_gather(hidden_local, 'fsdp', axis=2, tiled=True)  32 us
    all_to_all x1, waiting for transfers between devices, per_device(): lax.all_to_all(sent_rows.reshape(groups, slots, feat_local), 'expert', sp...  19.8 us
  transfers between devices with their start and end apart: 6, of which 4 were waited for; matrix products, arithmetic and copies ran while one was open for 18% of the time, Pallas kernels for 0%

commit v1 on v0

v1 whole, which is shorter than its diff:
```python
import functools

import jax
import jax.numpy as jnp
from jax import lax
from jax.experimental import pallas as pl
from jax.experimental.pallas import tpu as pltpu
from jax.sharding import PartitionSpec as P

BETA_ONE = 0.9
BETA_TWO = 0.999
BETA_THREE = 0.9999
EPS_ONE = 1e-30
EPS_TWO = 1e-16
CLIP_LIMIT = 1.0
LEARN_RATE = 0.01

MESH = pl.DeviceIdType.MESH
F32 = jnp.float32
BF16 = jnp.bfloat16
NE = 32
CAP = 8
SIDE = 4
T = 32
DL = 256
FF = 768
ROWS = NE * CAP
TILE = ROWS // (SIDE * SIDE)
COLS = 3 * FF
NSTAT = 1280
HALF = COLS // 2


def nn(a, b):
    return jnp.dot(a, b, preferred_element_type=F32)


def nt(a, b):
    return lax.dot_general(a, b, (((1,), (1,)), ((), ())), preferred_element_type=F32)


def tn(a, b):
    return lax.dot_general(a, b, (((0,), (0,)), ((), ())), preferred_element_type=F32)


def iota(shape, dim):
    return lax.broadcasted_iota(jnp.int32, shape, dim)


def one_hot(cond):
    return jnp.where(cond, 1.0, 0.0).astype(BF16)


def to_column(v):
    n = v.shape[1]
    return jnp.sum(jnp.where(iota((n, n), 0) == iota((n, n), 1), v, 0.0), axis=1, keepdims=True)


def to_row(v):
    n = v.shape[0]
    return jnp.sum(jnp.where(iota((n, n), 0) == iota((n, n), 1), v, 0.0), axis=0, keepdims=True)


def pack(rows):
    n = rows.shape[0] // CAP
    left = rows[:, :128].reshape(n, CAP, 128)
    right = rows[:, 128:].reshape(n, CAP, 128)
    return jnp.concatenate([left, right], axis=1).astype(BF16)


def unpack(blocks):
    wide = blocks.astype(F32)
    n = wide.shape[0]
    left = wide[:, :CAP].reshape(n * CAP, 128)
    right = wide[:, CAP:].reshape(n * CAP, 128)
    return jnp.concatenate([left, right], axis=1).astype(BF16)


def all_of(view, sem):
    pltpu.make_async_copy(view, view, sem).wait()


def main_kernel(
    mark,
    tokens, cotangent, ids, logits, plan, w_in, w_out, mom_in, mom_out, in_rows, out_cols,
    output, grad_tokens, grads, w_cat, m_cat, sums, row_v,
    send_x, send_c, recv_x, recv_c, x_rows, c_rows, x_t, c_t, parts, got_a, got_b, mid_a, mid_b, acc_a, acc_b,
    last_a, last_b, units, send_o, send_i, recv_o, recv_i, recv_o1, recv_i1, pick, pick1, gated, gated1,
    stat, stat_x, stat_y, pre_tile, ssem, rsem,
):
    me = lax.axis_index("expert")
    fs = lax.axis_index("fsdp")
    my, mx = fs // SIDE, lax.rem(fs, SIDE)
    stride, off = (1, 0) if mark is None else (NE // 4, mark)
    n_hot = NE // stride
    hot = None if mark is None else lax.rem(me, stride) == off

    def when_hot(f):
        if hot is None:
            f()
        else:
            pl.when(hot)(f)

    def both(f):
        f(0)
        when_hot(lambda: f(1))

    def x_peer(d):
        return (me, my * SIDE + lax.rem(mx + d, SIDE))

    def y_peer(d):
        return (me, lax.rem(my + d, SIDE) * SIDE + mx)

    def remote(src, dst, k, dev):
        pltpu.make_async_remote_copy(
            src_ref=src, dst_ref=dst, send_sem=ssem.at[k], recv_sem=rsem.at[k],
            device_id=dev, device_id_type=MESH,
        ).start()

    barrier = pltpu.get_barrier_semaphore()

    @pl.loop(1, NE)
    def _(i):
        pl.semaphore_signal(
            barrier, inc=1, device_id=(lax.rem(me + i, NE), fs), device_id_type=MESH
        )

    for d in range(1, SIDE):
        pl.semaphore_signal(barrier, inc=1, device_id=x_peer(d), device_id_type=MESH)
        pl.semaphore_signal(barrier, inc=1, device_id=y_peer(d), device_id_type=MESH)

    expert = iota((NE, T), 0)
    chosen = jnp.zeros((NE, T), F32)
    gate_of = jnp.zeros((NE, T), F32)
    sig = jax.nn.sigmoid(logits[...])
    gates = sig / jnp.sum(sig, axis=0, keepdims=True)
    picks = ids[...]
    for k in range(ids.shape[0]):
        hit = picks[k : k + 1, :] == expert
        chosen = jnp.where(hit, 1.0, chosen)
        gate_of = jnp.where(hit, gates[k : k + 1, :], gate_of)
    earlier = one_hot(iota((T, T), 0) < iota((T, T), 1))
    rank = jnp.where(chosen > 0.0, nn(chosen.astype(BF16), earlier), 1e6)
    marked = jnp.sum(
        jnp.where(iota((NE, NE), 0) == iota((NE, NE), 1), plan[...], 0), axis=1, keepdims=True
    )
    rank_hot = jnp.where(marked > 0, rank - CAP, 1e6)

    def selection(rank_block, gate_block, pick_ref, gated_ref, sx, sc):
        n = rank_block.shape[0]
        slot = iota((n, CAP, T), 1).astype(F32)
        sel = jnp.where(rank_block[:, None, :] == slot, 1.0, 0.0)
        wsel = (sel * gate_block[:, None, :]).reshape(n * CAP, T)
        sel = sel.reshape(n * CAP, T)
        pick_ref[...] = sel
        gated_ref[...] = wsel
        sel16 = sel.astype(BF16)
        sx[0:n] = pack(nn(sel16, tokens[...]))
        sc[0:n] = pack(nn(sel16, cotangent[...]) * jnp.sum(wsel, axis=1, keepdims=True))

    selection(rank, gate_of, pick, gated, send_x.at[0], send_c.at[0])
    if mark is None:
        rank1, gate1 = rank_hot, gate_of
    else:
        rank1 = jnp.concatenate([rank_hot[e : e + 1] for e in range(off, NE, stride)], axis=0)
        gate1 = jnp.concatenate([gate_of[e : e + 1] for e in range(off, NE, stride)], axis=0)
    selection(rank1, gate1, pick1, gated1, send_x.at[1], send_c.at[1])

    pl.semaphore_wait(barrier, NE - 1 + 2 * (SIDE - 1))

    def dispatch(src, dst, k):
        pltpu.make_async_copy(src.at[0, me], dst.at[0, me], rsem.at[k]).start()

        @pl.loop(1, NE)
        def _(i):
            to = lax.rem(me + i, NE)
            remote(src.at[0, to], dst.at[0, me], k, (to, fs))

        @pl.loop(0, n_hot)
        def _(i):
            r = lax.rem(i + me, n_hot)
            to = r * stride + off

            @pl.when(to == me)
            def _():
                pltpu.make_async_copy(src.at[1, r], dst.at[1, me], rsem.at[k + 1]).start()

            @pl.when(to != me)
            def _():
                remote(src.at[1, r], dst.at[1, me], k + 1, (to, fs))

    dispatch(send_x, recv_x, 0)
    dispatch(send_c, recv_c, 2)

    even = one_hot(iota((DL, 2 * DL), 1) == 2 * iota((DL, 2 * DL), 0))
    odd = one_hot(iota((DL, 2 * DL), 1) == 2 * iota((DL, 2 * DL), 0) + 1)
    eye = one_hot(iota((DL, DL), 0) == iota((DL, DL), 1))

    def split(w2, w3, into):
        flat = w2.reshape(2 * DL, FF)

        @pl.loop(0, FF // 256)
        def _(c):
            c0 = pl.multiple_of(c * 256, 256)
            piece = flat[:, pl.ds(c0, 256)]
            into[:, pl.ds(c0, 256)] = nn(even, piece).astype(BF16)
            into[:, pl.ds(c0 + FF, 256)] = nn(odd, piece).astype(BF16)
            into[:, pl.ds(c0 + 2 * FF, 256)] = nt(eye, w3[0, pl.ds(c0, 256), :]).astype(BF16)

    split(w_in, w_out, w_cat)

    def part_cols(q):
        return (0, FF) if q == 0 else (2 * FF, FF // 2)

    def got_cols(q):
        return (0, FF) if q == 0 else (FF, FF // 2)

    def project(b, q):
        src, rows_ref, t_ref = (recv_x, x_rows, x_t) if q == 0 else (recv_c, c_rows, c_t)
        all_of(src.at[b], rsem.at[2 * q + b])
        rows = unpack(src[b])
        rows_ref[b] = rows
        start, width = part_cols(q)

        @pl.loop(0, 2 * width // 256)
        def _(c):
            c0 = pl.multiple_of(start + c * 256, 256)
            piece = nn(rows_ref[b], w_cat[:, pl.ds(c0, 256)])
            parts[b, :, :, :, pl.ds(c0, 256)] = piece.reshape(SIDE, SIDE, TILE, 256).astype(BF16)

        g0, _w = got_cols(q)
        for d in range(1, SIDE):
            to_x, to_y = lax.rem(mx + d, SIDE), lax.rem(my + d, SIDE)
            remote(
                parts.at[b, :, to_x, :, pl.ds(start, width)],
                got_a.at[b, d - 1, :, :, pl.ds(g0, width)], 8 + 4 * q + 2 * b, x_peer(d),
            )
            remote(
                parts.at[b, to_y, :, :, pl.ds(start + width, width)],
                got_b.at[b, d - 1, :, :, pl.ds(g0, width)], 9 + 4 * q + 2 * b, y_peer(d),
            )

    def halfway(b, q):
        start, width = part_cols(q)
        g0, _w = got_cols(q)
        cols = pl.ds(g0, width)
        for half in range(2):
            got, mid, acc, last = (
                (got_a, mid_a, acc_a, last_a) if half == 0 else (got_b, mid_b, acc_b, last_b)
            )
            k = 8 + 4 * q + 2 * b + half
            all_of(got.at[b, :, :, :, cols], rsem.at[k])
            if half == 0:
                own = parts[b, :, mx, :, pl.ds(start, width)]
            else:
                own = parts[b, my, :, :, pl.ds(start + width, width)]
            total = own.astype(F32)
            for d in range(SIDE - 1):
                total = total + got[b, d, :, :, cols].astype(F32)
            acc[b, :, :, cols] = total
            mid[b, :, :, cols] = total.astype(BF16)
            for d in range(1, SIDE):
                to = lax.rem((my if half == 0 else mx) + d, SIDE)
                remote(
                    mid.at[b, to, :, cols], last.at[b, d - 1, :, cols], k + 8,
                    y_peer(d) if half == 0 else x_peer(d),
                )

    def finished(b, q, half):
        g0, width = got_cols(q)
        cols = pl.ds(g0, width)
        acc, last = (acc_a, last_a) if half == 0 else (acc_b, last_b)
        all_of(last.at[b, :, :, cols], rsem.at[16 + 4 * q + 2 * b + half])
        total = acc[b, my if half == 0 else mx, :, cols]
        for d in range(SIDE - 1):
            total = total + last[b, d, :, cols].astype(F32)
        return total

    def unit_cols(q):
        return (2 * FF, FF // 2) if q == 0 else (0, FF)

    def share(b, q):
        c0, width = unit_cols(q)
        first, second = pl.ds(c0, width), pl.ds(c0 + width, width)
        for d in range(1, SIDE):
            a, z = units.at[b, my, mx, :, first], units.at[b, my, mx, :, second]
            remote(a, a, 24 + 4 * q + 2 * b, y_peer(d))
            remote(z, z, 25 + 4 * q + 2 * b, x_peer(d))

    def spread(b, q):
        c0, width = unit_cols(q)
        first, second = pl.ds(c0, width), pl.ds(c0 + width, width)
        k = 24 + 4 * q + 2 * b
        all_of(units.at[b, 0:3, 0, :, first], rsem.at[k])
        a = units.at[b, :, mx, :, first]
        for d in range(1, SIDE):
            remote(a, a, k + 8, x_peer(d))
        all_of(units.at[b, 0, 0:3, :, second], rsem.at[k + 1])
        z = units.at[b, my, :, :, second]
        for d in range(1, SIDE):
            remote(z, z, k + 9, y_peer(d))

    def gathered(b, q):
        c0, width = unit_cols(q)
        for half in range(2):
            all_of(
                units.at[b, :, 0:3, :, pl.ds(c0 + half * width, width)],
                rsem.at[32 + 4 * q + 2 * b + half],
            )

    def forward(b):
        gate_pre, up_pre = finished(b, 0, 0), finished(b, 0, 1)
        s = jax.nn.sigmoid(gate_pre)
        pre_tile[b, 0] = gate_pre
        pre_tile[b, 1] = up_pre
        units[b, my, mx, :, 2 * FF : 3 * FF] = (gate_pre * s * up_pre).astype(BF16)
        share(b, 0)

    def backward(b):
        hidden_grad = jnp.concatenate([finished(b, 1, 0), finished(b, 1, 1)], axis=1)
        gate_pre, up_pre = pre_tile[b, 0], pre_tile[b, 1]
        s = jax.nn.sigmoid(gate_pre)
        gate_grad = hidden_grad * up_pre * s * (1.0 + gate_pre * (1.0 - s))
        units[b, my, mx, :, 0:FF] = gate_grad.astype(BF16)
        units[b, my, mx, :, FF : 2 * FF] = (hidden_grad * gate_pre * s).astype(BF16)
        share(b, 1)

    def give_back(b, src, dst0, dst1, k):
        if b == 0:
            pltpu.make_async_copy(src.at[0, me], dst0.at[me], rsem.at[k]).start()
        else:
            pltpu.make_async_copy(src.at[1, me], dst1.at[me // stride], rsem.at[k + 1]).start()

        @pl.loop(1, NE)
        def _(i):
            to = lax.rem(me + i, NE)
            if b == 0:
                remote(src.at[0, to], dst0.at[me], k, (to, fs))
            else:
                remote(src.at[1, to], dst1.at[me // stride], k + 1, (to, fs))

    def rows_of(b, start, width):
        return units[b, :, :, :, start : start + width].reshape(ROWS, width)

    def down(b):
        gathered(b, 0)
        out = nt(rows_of(b, 2 * FF, FF), w_cat[:, 2 * FF : 3 * FF])
        send_o[b] = pack(out)
        give_back(b, send_o, recv_o, recv_o1, 40)

    def up(b):
        gathered(b, 1)
        out = nt(rows_of(b, 0, 2 * FF), w_cat[:, 0 : 2 * FF])
        send_i[b] = pack(out)
        give_back(b, send_i, recv_i, recv_i1, 42)

    both(lambda b: project(b, 0))
    both(lambda b: project(b, 1))
    split(mom_in, mom_out, m_cat)
    both(lambda b: halfway(b, 0))
    both(lambda b: halfway(b, 1))
    both(forward)
    both(backward)

    def transposes(b):
        x_t[b] = x_rows[b].astype(F32).T.astype(BF16)
        c_t[b] = c_rows[b].astype(F32).T.astype(BF16)

    both(transposes)
    both(lambda b: spread(b, 0))
    both(lambda b: spread(b, 1))
    both(down)
    both(up)

    def gradients(b):
        @pl.loop(0, COLS // 256)
        def _(c):
            cols = pl.ds(pl.multiple_of(c * 256, 256), 256)
            right = units[b, :, :, :, cols].reshape(ROWS, 256)

            def put(left):
                g = nn(left, right)
                if b == 0:
                    grads[:, cols] = g
                else:
                    grads[:, cols] = grads[:, cols] + g

            @pl.when(c < 2 * FF // 256)
            def _():
                put(x_t[b])

            @pl.when(c >= 2 * FF // 256)
            def _():
                put(c_t[b])

    both(gradients)

    def square_rows(c0, n):
        def step(c, total):
            g = grads[:, pl.ds(pl.multiple_of(c0 + c * 128, 128), 128)]
            return total + g * g

        total = lax.fori_loop(0, n // 128, step, jnp.zeros((DL, 128), F32))
        return jnp.sum(total, axis=1, keepdims=True) / n + EPS_ONE

    kept_in = to_column(in_rows[0, 0:1, :])
    kept_out = to_column(out_cols[0, 0:1, :])
    v_in = BETA_TWO * kept_in + (1.0 - BETA_TWO) * square_rows(0, 2 * FF)
    v_out = BETA_TWO * kept_out + (1.0 - BETA_TWO) * square_rows(2 * FF, FF)
    row_v[...] = jnp.where(iota((DL, 128), 1) == 0, v_in, v_out)
    root_in, root_out = lax.rsqrt(v_in), lax.rsqrt(v_out)

    def column_sums(c, carry):
        cols = pl.ds(pl.multiple_of(c * 128, 128), 128)
        g = grads[:, cols]
        m = m_cat[:, cols].astype(F32)
        r = jnp.where(c < 2 * FF // 128, root_in, root_out)
        gr = g * r
        four = [jnp.sum(v, axis=0, keepdims=True) for v in (g * g, gr * gr, gr * m, m * m)]
        low = c >= HALF // 128
        at = pl.ds(pl.multiple_of((c - jnp.where(low, HALF // 128, 0)) * 128, 128), 128)
        block = jnp.concatenate(four, axis=0)

        @pl.when(low)
        def _():
            stat[4:8, at] = block

        @pl.when(jnp.logical_not(low))
        def _():
            stat[0:4, at] = block

        return carry

    lax.fori_loop(0, COLS // 128, column_sums, 0)
    total_v = jnp.sum(v_in, axis=0, keepdims=True)
    total_r = jnp.sum(in_rows[0, 1:2, :], axis=1, keepdims=True)
    stat[:, HALF:NSTAT] = jnp.where(iota((8, NSTAT - HALF), 0) == 0, total_v, total_r)

    mid = NSTAT // 2
    one, two = pl.ds(0, mid), pl.ds(mid, mid)
    stat_x[mx, :, one] = stat[:, one]
    stat_y[my, :, two] = stat[:, two]
    for d in range(1, SIDE):
        remote(stat.at[:, one], stat_x.at[mx, :, one], 44, x_peer(d))
        remote(stat.at[:, two], stat_y.at[my, :, two], 45, y_peer(d))
    all_of(stat_x.at[0:3, :, one], rsem.at[44])
    part = stat_x[0, :, one] + stat_x[1, :, one] + stat_x[2, :, one] + stat_x[3, :, one]
    stat_y[my, :, one] = part
    for d in range(1, SIDE):
        mine = stat_y.at[my, :, one]
        remote(mine, mine, 46, y_peer(d))
    all_of(stat_y.at[0:3, :, two], rsem.at[45])
    part = stat_y[0, :, two] + stat_y[1, :, two] + stat_y[2, :, two] + stat_y[3, :, two]
    stat_x[mx, :, two] = part
    for d in range(1, SIDE):
        mine = stat_x.at[mx, :, two]
        remote(mine, mine, 47, x_peer(d))

    def combine(weights, recv, exact):
        rows = unpack(recv[...])
        if exact:
            return tn(weights.astype(BF16), rows)
        high = weights.astype(BF16)
        low = (weights - high.astype(F32)).astype(BF16)
        return tn(high, rows) + tn(low, rows)

    all_of(recv_o, rsem.at[40])
    all_of(recv_o1, rsem.at[41])
    output[...] = (
        combine(gated[...], recv_o, False) + combine(gated1[...], recv_o1, False)
    ).astype(BF16)
    all_of(recv_i, rsem.at[42])
    all_of(recv_i1, rsem.at[43])
    grad_tokens[...] = (
        combine(pick[...], recv_i, True) + combine(pick1[...], recv_i1, True)
    ).astype(BF16)

    all_of(stat_y.at[0:3, :, one], rsem.at[46])
    sums[:, one] = stat_y[0, :, one] + stat_y[1, :, one] + stat_y[2, :, one] + stat_y[3, :, one]
    all_of(stat_x.at[0:3, :, two], rsem.at[47])
    sums[:, two] = stat_x[0, :, two] + stat_x[1, :, two] + stat_x[2, :, two] + stat_x[3, :, two]

    for q, src in ((0, send_x), (1, send_c)):
        all_of(src.at[0, 0 : NE - 1], ssem.at[2 * q])
        if mark is None:
            all_of(src.at[1, 0 : NE - 1], ssem.at[2 * q + 1])
        else:
            pl.when(hot)(lambda: all_of(src.at[1, 0 : n_hot - 1], ssem.at[2 * q + 1]))
            pl.when(jnp.logical_not(hot))(lambda: all_of(src.at[1, 0:n_hot], ssem.at[2 * q + 1]))

    def sent(b):
        for q in range(2):
            _s, width = part_cols(q)
            g0, _w = got_cols(q)
            c0, uw = unit_cols(q)
            cols = pl.ds(g0, width)
            for half in range(2):
                k = 4 * q + 2 * b + half
                got, last = (got_a, last_a) if half == 0 else (got_b, last_b)
                all_of(got.at[b, :, :, :, cols], ssem.at[8 + k])
                all_of(last.at[b, :, :, cols], ssem.at[16 + k])
                ucols = pl.ds(c0 + half * uw, uw)
                all_of(units.at[b, 0, 0:3, :, ucols], ssem.at[24 + k])
                all_of(units.at[b, :, 0:3, :, ucols], ssem.at[32 + k])
        all_of(send_o.at[b, 0 : NE - 1], ssem.at[40 + b])
        all_of(send_i.at[b, 0 : NE - 1], ssem.at[42 + b])

    both(sent)
    for k in range(4):
        all_of(stat_x.at[0:3, :, one], ssem.at[44 + k])


def update_kernel(
    grads, w_cat, m_cat, sums, row_v, out16, grad16, in_rows, in_cols, out_rows, out_cols,
    output, grad_tokens, new_w_in, new_w_out, new_mom_in, new_mom_out,
    new_in_rows, new_in_cols, new_out_rows, new_out_cols, moment, w16, m16,
):
    output[...] = out16[...]
    grad_tokens[...] = grad16[...]
    full = DL * SIDE * SIDE
    n_in, n_out = 2 * FF, FF

    def line(k):
        return jnp.concatenate([sums[k : k + 1, 0:HALF], sums[4 + k : 5 + k, 0:HALF]], axis=1)

    sq, sq_scaled, cross, sq_mom = line(0), line(1), line(2), line(3)
    sum_v = sums[0:1, HALF : HALF + 1]
    sum_r = sums[1:2, HALF : HALF + 1]

    def state(k):
        return jnp.concatenate(
            [in_cols[0, k, 0:1, :], in_cols[0, k, 1:2, :], out_rows[0, k : k + 1, :]], axis=1
        )

    v_in, v_out = row_v[:, 0:1], row_v[:, 1:2]
    col_v = BETA_TWO * state(0) + (1.0 - BETA_TWO) * (sq / full + EPS_ONE)
    is_in = iota((1, COLS), 1) < n_in

    def total(v):
        low = jnp.sum(v[:, 0:n_in], axis=1, keepdims=True)
        return low, jnp.sum(v[:, n_in:COLS], axis=1, keepdims=True)

    mean_in = sum_v / full
    mean_out = total(col_v)[1] / n_out
    inv = 1.0 / col_v
    norm_in, norm_out = total(sq_scaled * inv)
    clip_in = jnp.maximum(1.0, jnp.sqrt(norm_in * mean_in / (full * n_in)) / CLIP_LIMIT)
    clip_out = jnp.maximum(1.0, jnp.sqrt(norm_out * mean_out / (full * n_out)) / CLIP_LIMIT)
    scale = jnp.where(is_in, jnp.sqrt(mean_in) / clip_in, jnp.sqrt(mean_out) / clip_out)
    col_s = scale * lax.rsqrt(col_v)
    keep = BETA_ONE * BETA_ONE
    residue = keep * (col_s * col_s * sq_scaled - 2.0 * col_s * cross + sq_mom) + full * EPS_TWO
    col_r = BETA_THREE * state(1) + (1.0 - BETA_THREE) * residue / full
    mean_r_in = BETA_THREE * sum_r / full + (1.0 - BETA_THREE) * total(residue)[0] / (full * n_in)
    mean_r_out = total(col_r)[1] / n_out
    root_in, root_out = lax.rsqrt(v_in), lax.rsqrt(v_out)

    def first(c0, root, scale_row):
        acc = jnp.zeros((DL, 128), F32)
        for c in range(scale_row.shape[1] // 128):
            cols = slice(c0 + c * 128, c0 + (c + 1) * 128)
            u = grads[:, cols] * root * scale_row[:, c * 128 : (c + 1) * 128]
            old = m_cat[:, cols].astype(F32)
            new = BETA_ONE * old + (1.0 - BETA_ONE) * u
            diff = u - new
            acc = acc + (diff * diff + EPS_TWO)
            moment[:, cols] = new
            m16[:, cols] = new.astype(BF16)
        return jnp.sum(acc, axis=1, keepdims=True)

    res_in = first(0, root_in, col_s[:, 0:n_in])
    res_out = first(n_in, root_out, col_s[:, n_in:COLS])
    r_in = (
        BETA_THREE * to_column(in_rows[0, 1:2, :]) + (1.0 - BETA_THREE) * res_in / n_in
    )
    r_out = (
        BETA_THREE * to_column(out_cols[0, 1:2, :]) + (1.0 - BETA_THREE) * res_out / n_out
    )
    step_in, step_out = LEARN_RATE * lax.rsqrt(r_in), LEARN_RATE * lax.rsqrt(r_out)
    col_step = lax.rsqrt(col_r) * jnp.where(is_in, jnp.sqrt(mean_r_in), jnp.sqrt(mean_r_out))
    for c in range(COLS // 128):
        cols = slice(c * 128, (c + 1) * 128)
        rows = step_in if c < n_in // 128 else step_out
        w16[:, cols] = (
            w_cat[:, cols].astype(F32) - moment[:, cols] * rows * col_step[:, cols]
        ).astype(BF16)

    even = one_hot(iota((2 * DL, DL), 0) == 2 * iota((2 * DL, DL), 1))
    odd = one_hot(iota((2 * DL, DL), 0) == 2 * iota((2 * DL, DL), 1) + 1)
    eye = one_hot(iota((DL, DL), 0) == iota((DL, DL), 1))
    for src, inner, outer in ((w16, new_w_in, new_w_out), (m16, new_mom_in, new_mom_out)):
        flat = inner.reshape(2 * DL, FF)
        for c in range(FF // 256):
            lo = slice(c * 256, (c + 1) * 256)
            hi = slice(FF + c * 256, FF + (c + 1) * 256)
            flat[:, lo] = (nn(even, src[:, lo]) + nn(odd, src[:, hi])).astype(BF16)
            third = slice(2 * FF + c * 256, 2 * FF + (c + 1) * 256)
            outer[0, lo, :] = nt(eye, src[:, third]).astype(BF16)

    new_in_rows[0, 0:1, :] = to_row(v_in)
    new_in_rows[0, 1:2, :] = to_row(r_in)
    new_out_cols[0, 0:1, :] = to_row(v_out)
    new_out_cols[0, 1:2, :] = to_row(r_out)
    for k, v in ((0, col_v), (1, col_r)):
        new_in_cols[0, k, 0:1, :] = v[:, 0:FF]
        new_in_cols[0, k, 1:2, :] = v[:, FF : 2 * FF]
        new_out_rows[0, k : k + 1, :] = v[:, 2 * FF :]


def vmem():
    return pl.BlockSpec(memory_space=pltpu.VMEM)


def main_call(mark, *operands):
    n_hot = NE if mark is None else 4
    sds = jax.ShapeDtypeStruct
    outs = (
        sds((T, DL), BF16),
        sds((T, DL), BF16),
        sds((DL, COLS), F32),
        sds((DL, COLS), BF16),
        sds((DL, COLS), BF16),
        sds((8, NSTAT), F32),
        sds((DL, 128), F32),
    )
    block = (2, NE, 2 * CAP, 128)
    wide = COLS // 2
    scratch = [
        pltpu.VMEM(block, BF16),
        pltpu.VMEM(block, BF16),
        pltpu.VMEM(block, BF16),
        pltpu.VMEM(block, BF16),
        pltpu.VMEM((2, ROWS, DL), BF16),
        pltpu.VMEM((2, ROWS, DL), BF16),
        pltpu.VMEM((2, DL, ROWS), BF16),
        pltpu.VMEM((2, DL, ROWS), BF16),
        pltpu.VMEM((2, SIDE, SIDE, TILE, COLS), BF16),
        pltpu.VMEM((2, SIDE - 1, SIDE, TILE, wide), BF16),
        pltpu.VMEM((2, SIDE - 1, SIDE, TILE, wide), BF16),
        pltpu.VMEM((2, SIDE, TILE, wide), BF16),
        pltpu.VMEM((2, SIDE, TILE, wide), BF16),
        pltpu.VMEM((2, SIDE, TILE, wide), F32),
        pltpu.VMEM((2, SIDE, TILE, wide), F32),
        pltpu.VMEM((2, SIDE - 1, TILE, wide), BF16),
        pltpu.VMEM((2, SIDE - 1, TILE, wide), BF16),
        pltpu.VMEM((2, SIDE, SIDE, TILE, COLS), BF16),
        pltpu.VMEM(block, BF16),
        pltpu.VMEM(block, BF16),
        pltpu.VMEM((NE, 2 * CAP, 128), BF16),
        pltpu.VMEM((NE, 2 * CAP, 128), BF16),
        pltpu.VMEM((n_hot, 2 * CAP, 128), BF16),
        pltpu.VMEM((n_hot, 2 * CAP, 128), BF16),
        pltpu.VMEM((ROWS, T), F32),
        pltpu.VMEM((n_hot * CAP, T), F32),
        pltpu.VMEM((ROWS, T), F32),
        pltpu.VMEM((n_hot * CAP, T), F32),
        pltpu.VMEM((8, NSTAT), F32),
        pltpu.VMEM((SIDE, 8, NSTAT), F32),
        pltpu.VMEM((SIDE, 8, NSTAT), F32),
        pltpu.VMEM((2, 2, TILE, FF), F32),
        pltpu.SemaphoreType.DMA((48,)),
        pltpu.SemaphoreType.DMA((48,)),
    ]
    return pl.pallas_call(
        functools.partial(main_kernel, mark),
        out_shape=outs,
        in_specs=[vmem()] * len(operands),
        out_specs=tuple(vmem() for _ in outs),
        scratch_shapes=scratch,
        compiler_params=pltpu.CompilerParams(
            collective_id=0 if mark is None else 1 + mark,
            has_side_effects=True,
            vmem_limit_bytes=48 * 2**20,
        ),
    )(*operands)


def per_device(
    tokens, cotangent, expert_ids, gate_logits, shadow_plan, w_in, w_out, mom_in, mom_out,
    in_rows, in_cols, out_rows, out_cols,
):
    operands = (
        tokens, cotangent, expert_ids.T, gate_logits.T, shadow_plan.reshape(1, -1),
        w_in, w_out, mom_in, mom_out, in_rows, out_cols,
    )
    out16, grad16, grads, w_cat, m_cat, sums, row_v = main_call(None, *operands)
    sds = jax.ShapeDtypeStruct
    outs = (
        sds(tokens.shape, BF16),
        sds(tokens.shape, BF16),
        sds(w_in.shape, BF16),
        sds(w_out.shape, BF16),
        sds(w_in.shape, BF16),
        sds(w_out.shape, BF16),
        sds(in_rows.shape, F32),
        sds(in_cols.shape, F32),
        sds(out_rows.shape, F32),
        sds(out_cols.shape, F32),
    )
    return pl.pallas_call(
        update_kernel,
        out_shape=outs,
        in_specs=[vmem()] * 11,
        out_specs=tuple(vmem() for _ in outs),
        scratch_shapes=[
            pltpu.VMEM((DL, COLS), F32),
            pltpu.VMEM((DL, COLS), BF16),
            pltpu.VMEM((DL, COLS), BF16),
        ],
        compiler_params=pltpu.CompilerParams(vmem_limit_bytes=48 * 2**20),
    )(grads, w_cat, m_cat, sums, row_v, out16, grad16, in_rows, in_cols, out_rows, out_cols)


def solution(mesh):
    both = P("expert", "fsdp")
    rows3 = P("expert", "fsdp", None, None)
    cols3 = P("expert", None, "fsdp")
    own = P("expert", None)
    return jax.shard_map(
        per_device,
        mesh=mesh,
        in_specs=(
            both, both, own, own, P(), rows3, cols3, rows3, cols3,
            cols3, P("expert", None, None, None), P("expert", None, None), cols3,
        ),
        out_specs=(
            both, both, rows3, cols3, rows3, cols3,
            cols3, P("expert", None, None, None), P("expert", None, None), cols3,
        ),
        check_vma=False,
    )
```

time: 582 us -> 109 us (0.19)
  the two profiles are of different devices: /device:TPU:32 before, /device:TPU:1 now
where the time goes in v1:
time: 109 us
  Pallas kernels  97.1 us (89%)
  local copies, waits for them, and re-layouts  10.7 us (10%)
    pallas_call x1, Pallas kernels, main_call(): pl.pallas_call(functools.partial(main_kernel, mark), out_shape=outs, in_s...  92.9 us
    unnamed x28, local copies, waits for them, and re-layouts  10.7 us
    pallas_call x1, Pallas kernels, per_device(): pl.pallas_call(update_kernel, out_shape=outs, in_specs=[vmem()] * 11, out...  4.24 us

profile of v1, /device:TPU:1, one launch (start us, length us, event | category | flops | bytes accessed | tf_op | source)
XLA Modules:
  0.0 108.6 jit_solution(80260417431467038)
XLA Ops:
  0.6 0.0 copy-start.1
  0.7 1.1 %copy-done.1 = bf16[1,256,2,768]{3,2,1,0:T(2,128)(2,1)S(1)} copy-done((bf16[1,256,2,768]{3,2,1,0:T(2,128)(2,1)S(1)}, bf16[1,256,2,768]{3,2,1,0:T(2,128)(2,1)}, u32[]{:S(2)}) %copy-start.1) | copy-done | bytes 786456
  1.8 0.0 copy-start.2
  1.8 1.1 %copy-done.2 = bf16[1,256,2,768]{3,2,1,0:T(2,128)(2,1)S(1)} copy-done((bf16[1,256,2,768]{3,2,1,0:T(2,128)(2,1)S(1)}, bf16[1,256,2,768]{3,2,1,0:T(2,128)(2,1)}, u32[]{:S(2)}) %copy-start.2) | copy-done | bytes 786456
  2.9 0.0 copy-start.3
  2.9 1.0 copy-done.3
  3.9 0.0 copy-start.4
  3.9 1.0 copy-done.4
  4.9 0.0 copy-start.5
  4.9 0.7 copy-done.5
  5.6 0.0 copy-start.6
  5.6 0.7 copy-done.6
  6.3 0.0 copy-start.8
  6.3 0.7 copy-done.8
  7.0 0.0 copy-start.9
  7.0 0.7 copy-done.9
  7.7 0.0 copy-start.11
  7.7 0.7 copy-done.11
  8.4 0.0 copy-start.12
  8.4 0.7 copy-done.12
  9.1 0.0 copy-start.13
  9.1 0.7 copy-done.13
  9.7 0.0 copy-start.7
  9.7 0.0 copy-start.10
  9.7 92.9 %shard_map.204 = (bf16[32,256]{1,0:T(8,128)(2,1)S(1)}, bf16[32,256]{1,0:T(8,128)(2,1)S(1)}, f32[256,2304]{1,0:T(8,128)}, bf16[256,2304]{1,0:T(8,128)(2,1)S(1)}, ...) custom-call(bf16[32,256]{1,0:T(8,128)(2,1)S(1)} %copy-done.5, ...), custom_call_target="tpu_custom_call" | custom-call | tf_op jit(solution)/shard_map/pallas_call | solution.py:664
  102.6 0.0 copy-done.7
  102.6 0.0 copy-done.10
  102.7 0.0 copy-start
  102.7 1.7 %copy-done = f32[256,2304]{1,0:T(8,128)S(1)} copy-done((f32[256,2304]{1,0:T(8,128)S(1)}, f32[256,2304]{1,0:T(8,128)}, u32[]{:S(2)}) %copy-start) | copy-done | bytes 2359320
  104.3 4.2 %shard_map.205 = (bf16[32,256]{1,0:T(8,128)(2,1)}, bf16[32,256]{1,0:T(8,128)(2,1)}, bf16[1,256,2,768]{3,2,1,0:T(2,128)(2,1)}, bf16[1,768,256]{2,1,0:T(8,128)(2,1...) custom-call(f32[256,2304]{1,0:T(8,128)S(1)} %copy-done, ...), custom_call_target="tpu_custom_call" | custom-call | tf_op jit(solution)/shard_map/pallas_call | solution.py:700
Async XLA Ops:
  0.6 1.1 %copy-start.1 = (bf16[1,256,2,768]{3,2,1,0:T(2,128)(2,1)S(1)}, bf16[1,256,2,768]{3,2,1,0:T(2,128)(2,1)}, u32[]{:S(2)}) copy-start(bf16[1,256,2,768]{3,2,1,0:T(2,128)(2,1)} %w_in.1) | copy-start | bytes 2359300
  1.8 1.1 %copy-start.2 = (bf16[1,256,2,768]{3,2,1,0:T(2,128)(2,1)S(1)}, bf16[1,256,2,768]{3,2,1,0:T(2,128)(2,1)}, u32[]{:S(2)}) copy-start(bf16[1,256,2,768]{3,2,1,0:T(2,128)(2,1)} %mom_in.1) | copy-start | bytes 2359300
  2.9 1.0 copy-start.3
  3.9 1.0 copy-start.4
  4.9 0.7 copy-start.5
  5.6 0.7 copy-start.6
  6.3 0.7 copy-start.8
  7.0 0.7 copy-start.9
  7.7 0.7 copy-start.11
  8.4 0.7 copy-start.12
  9.1 0.7 copy-start.13
  9.7 92.9 %copy-start.7 = (f32[1,2,2,768]{3,2,1,0:T(2,128)S(1)}, f32[1,2,2,768]{3,2,1,0:T(2,128)}, u32[]{:S(2)}) copy-start(f32[1,2,2,768]{3,2,1,0:T(2,128)} %in_cols.1) | copy-start | bytes 36868
  9.7 92.9 %copy-start.10 = (f32[1,2,768]{2,1,0:T(2,128)S(1)}, f32[1,2,768]{2,1,0:T(2,128)}, u32[]{:S(2)}) copy-start(f32[1,2,768]{2,1,0:T(2,128)} %out_rows.1) | copy-start | bytes 18436
  102.7 1.7 %copy-start = (f32[256,2304]{1,0:T(8,128)S(1)}, f32[256,2304]{1,0:T(8,128)}, u32[]{:S(2)}) copy-start(f32[256,2304]{1,0:T(8,128)} %get-tuple-element.17.grads) | copy-start | bytes 7077892
